TPU v7x, 256 devices: a whole 4x4x8 slice. The times are simulated.
256 devices in a mesh: req: 16 (over x, z_lo), patch: 16 (over z_hi, y, core).
Axes of the slice: x: 4, y: 4, z: 8 (z_hi: 2, z_lo: 4; z = z_hi * 4 + z_lo), core: 2. Of those that a mesh axis runs over, the one named last changes fastest.
Arguments:
- tokens: bfloat16 [16, 2048, 3072], P('req', 'patch'), may hold values from -28 to 28, as said below
- projection_weight: bfloat16 [3072, 16, 384], P(None, 'patch'), may hold values from -0.109375 to 0.109375
- projection_bias: bfloat16 [16, 384], P('patch'), may hold values from -3 to 3
- adapter_down_weight: bfloat16 [16, 3072, 32], P('req'), may hold values from -0.109375 to 0.109375
- adapter_up_weight: bfloat16 [16, 32, 16, 384], P('req', None, 'patch'), may hold values from -1 to 1
- tile_allow_mask: int32 [16, 16, 32], P('req'), may hold values 0 or 1
- references: int32 [4], replicated, may hold values from 0 to 15, as said below
- pairing: int32 [16], replicated, may hold values from 0 to 3
Outputs:
- mixed: bfloat16 [16, 2048, 2048], P('req', 'patch')
Inputs may be any that keep to these rules, and one draw needn't show every extreme that they name: Draws of tokens stay in this range. `references`: 4 distinct request indices; the last request is always one of them.
All inputs are finite; a program needn't handle non-finite values. No bound on the sum of `tile_allow_mask` on one device may be relied on, other than what follows from the above.
Results may differ from a plain program's by a relative error of at most 0.04.
Values may be sent and summed in bfloat16 or wider, within the bound.
A program may use at most 64 MiB of HBM per device.

v0:
```python
import jax
import jax.numpy as jnp
from jax import lax
from jax.sharding import PartitionSpec as P

TILE = 128


def shortened(array):

    def short(part):
        return part.astype(jnp.bfloat16) if part.dtype == jnp.float32 else part

    return jax.tree.map(short, array)


def on_device(
    tokens,
    projection_weight,
    projection_bias,
    adapter_down_weight,
    adapter_up_weight,
    tile_allow_mask,
    references,
    pairing,
):
    own_tokens = tokens[0]
    local_down_matrix = adapter_down_weight[0]
    local_up_matrix = adapter_up_weight[0]
    bias_f32 = projection_bias.astype(jnp.float32)
    token_rows = lax.all_gather(own_tokens, "patch", axis=0, tiled=True)
    lowrank = jnp.dot(token_rows, local_down_matrix, preferred_element_type=jnp.float32).astype(
        jnp.bfloat16
    )
    base_part = jnp.einsum(
        "td,dhe->the", token_rows, projection_weight, preferred_element_type=jnp.float32
    )
    lowrank_part = jnp.einsum(
        "tr,rhe->the", lowrank, local_up_matrix, preferred_element_type=jnp.float32
    )
    projected_rows = (base_part + lowrank_part + bias_f32).astype(jnp.bfloat16)
    head_size = projection_weight.shape[2] // 3
    heads_here = projection_weight.shape[1]
    length = projected_rows.shape[0]
    queries = projected_rows[..., :head_size]
    own_pairs = projected_rows[..., head_size:]
    slot_index = lax.dynamic_index_in_dim(pairing, lax.axis_index("req"), 0, keepdims=False)
    owner_index = lax.dynamic_index_in_dim(references, slot_index, 0, keepdims=False)
    collected = lax.all_gather(own_pairs[None], "req", axis=0, tiled=True)
    paired = lax.dynamic_index_in_dim(collected, owner_index, 0, keepdims=False)
    key_pairs = jnp.concatenate([own_pairs, paired], 0)
    tile_count = tile_allow_mask.shape[1]
    rows_tile = lax.broadcasted_iota(jnp.int32, (tile_count, 2 * tile_count), 0)
    cols_tile = lax.broadcasted_iota(jnp.int32, (tile_count, 2 * tile_count), 1)
    tile_allow = (tile_allow_mask[0] == 1) | (rows_tile == cols_tile)
    wide_allow = jnp.repeat(tile_allow, TILE, axis=1)
    block_rows = min(512, length)
    score_scale = head_size ** (-0.5)

    def one_block(block_index):
        first_row = block_index * block_rows
        row_allow = jnp.repeat(
            lax.dynamic_slice_in_dim(wide_allow, first_row // TILE, block_rows // TILE, 0),
            TILE,
            axis=0,
        )
        query_block = lax.dynamic_slice_in_dim(queries, first_row, block_rows, 0)
        scores = (
            jnp.einsum(
                "qd,kd->qk",
                query_block[:, 0],
                key_pairs[:, 0, :head_size],
                preferred_element_type=jnp.float32,
            )
            * score_scale
        )
        scores = jnp.where(row_allow, scores, -jnp.inf)
        row_max = jnp.max(scores, axis=-1, keepdims=True)
        weights = jnp.exp(scores - row_max)
        row_total = jnp.sum(weights, axis=-1, keepdims=True)
        probability = (weights / row_total).astype(jnp.bfloat16)
        results = [
            jnp.dot(
                probability, key_pairs[:, 0, head_size:], preferred_element_type=jnp.float32
            ).astype(jnp.bfloat16)
        ]
        return jnp.concatenate(results, 1)

    blocks_out = lax.map(one_block, jnp.arange(length // block_rows, dtype=jnp.int32))
    mixed = blocks_out.reshape(length, heads_here * head_size)
    return lax.all_to_all(
        shortened(mixed), "patch", split_axis=0, concat_axis=1, tiled=True
    ).astype(mixed.dtype)[None]


def solution(mesh):
    in_specs = (
        P("req", "patch", None),
        P(None, "patch", None),
        P("patch", None),
        P("req", None, None),
        P("req", None, "patch", None),
        P("req", None, None),
        P(),
        P(),
    )
    out_specs = P("req", "patch", None)
    return jax.shard_map(
        on_device, mesh=mesh, in_specs=in_specs, out_specs=out_specs, check_vma=False
    )
```

profile of v0, /device:TPU:1, one launch (start us, length us, event | category | flops | bytes accessed | tf_op | source)
XLA Modules:
  0.0 604.7 jit_solution(257961988601979301)
XLA Ops:
  6.5 0.0 copy-start
  6.5 0.0 all-gather.5.cloned.1.call-start
  6.5 0.7 all-gather.5.cloned.1.call-update
  7.3 0.0 all-gather.7.cloned.1.call-start
  7.3 0.7 convert_reduce_fusion
  8.0 0.0 copy-start.3
  8.0 147.4 %all-gather.5.cloned.1.call-done = bf16[1,2048,3072]{2,1,0:T(8,128)(2,1)} async-done(((bf16[1,128,3072]{2,1,0:T(8,128)(2,1)}), bf16[1,2048,3072]{2,1,0:T(8,128)(2,1)}) %all-gather.5.cloned.1.call-update) | async-done | bytes 12582928 | tf_op jit(solution)/shard_map/all_gather | solution.py:31
  155.4 0.0 copy-done
  155.4 10.7 %fusion.14 = f32[2048,384]{1,0:T(8,128)} fusion(bf16[1,2048,3072]{2,1,0:T(8,128)(2,1)} %all-gather.5.cloned.1.call-done, bf16[3072,1,384]{2,0,1:T(8,128)(2,1)S(1)} %copy-done), kind=kOutput, calls=%fused_computation.19 | convolution fusion | flops 4831838208 | bytes 18087936 | tf_op jit(solution)/shard_map/td,dhe->the/dot_general | solution.py:35
  166.2 0.0 copy-done.2
  166.2 0.0 copy-done.3
  166.2 0.0 copy-start.6
  166.2 0.0 copy-start.4
  166.2 11.1 %fusion.16 = bf16[2048,1,384]{2,0,1:T(8,128)(2,1)} fusion(f32[2048,384]{1,0:T(8,128)} %fusion.14, bf16[1,2048,3072]{2,1,0:T(8,128)(2,1)} %all-gather.5.cloned.1.call-done, f32[384]{0:T(512)S(1)} %convert_reduce_fusion, bf16[1,3072,32]{1,2,0:T(8,128)(2,1)S(1)} %copy-done.2, bf16[1,32,1,384]{3,1,2,0:T(8,128)(2,1)S(1)} %copy-done.3), kind=kOutput, calls=%fused_computation.22 | convolution fusion | flops 455409664 | bytes 17524224 | tf_op jit(solution)/shard_map/tr,rhe->the/dot_general | solution.py:38
  177.3 2.3 slice.21
  179.6 0.0 all-gather.7.cloned.1.call-update
  179.6 0.0 copy-done.5
  179.6 0.6 dynamic_slice.31
  182.3 0.6 dynamic_slice.32
  184.3 0.1 broadcast_in_dim.36
  185.2 343.7 %all-gather.7.cloned.1.call-done = bf16[32768,1,256]{2,0,1:T(8,128)(2,1)} async-done(((bf16[2048,1,256]{2,0,1:T(8,128)(2,1)}), bf16[32768,1,256]{2,0,1:T(8,128)(2,1)}) %all-gather.7.cloned.1.call-update) | async-done | bytes 16777232 | tf_op jit(solution)/shard_map/all_gather | solution.py:49
  528.9 1.3 dynamic-slice_bitcast_fusion
  530.2 2.7 pad_maximum_fusion
  532.9 40.6 %while.12 = (s32[]{:T(128)}, bf16[4,512,128]{2,1,0:T(8,128)(2,1)S(1)}, s32[4]{0:T(128)S(1)}, pred[16,4096]{1,0:T(8,128)(4,1)S(1)}, bf16[2048,1,128]{2,0,1:T(8,12...) while((s32[]{:T(128)}, ...), condition=%wide.region_3.4_spmd, body=%wide.region_0.3_spmd.sunk | while | flops 1098972160 | bytes 44394908 | solution.py:89
  532.9 0.6 dynamic_slice.47
  534.3 2.7 fusion.35
  536.9 2.3 fusion.36
  539.2 2.5 divide_convert_fusion.2
  541.7 1.3 fusion.37
  543.0 0.7 dynamic_slice.47
  544.4 2.7 fusion.35
  547.1 2.3 fusion.36
  549.4 2.5 divide_convert_fusion.2
  551.9 0.0 copy-done.1
  551.9 1.3 fusion.37
  553.2 0.7 dynamic_slice.47
  554.6 2.7 fusion.35
  557.2 2.3 fusion.36
  559.6 2.5 divide_convert_fusion.2
  562.0 1.3 fusion.37
  563.4 0.7 dynamic_slice.47
  564.7 2.7 fusion.35
  567.4 2.3 fusion.36
  569.7 2.5 divide_convert_fusion.2
  572.2 1.3 fusion.37
  573.5 23.1 %all_to_all.16 = bf16[16,128,128]{2,1,0:T(8,128)(2,1)S(1)} all-to-all(bf16[16,128,128]{2,1,0:T(8,128)(2,1)S(1)} %bitcast.86), channel_id=1, replica_groups=mesh['req'=16,'patch'=16] {'patch'}, dimensions={0} | all-to-all | bytes 1048576 | tf_op jit(solution)/shard_map/all_to_all | solution.py:91
  596.6 0.3 copy.17
  596.9 1.0 copy.18
  (21 shorter events, 0.2 us)
Async XLA Ops:
  6.5 148.9 %copy-start = (bf16[3072,1,384]{2,0,1:T(8,128)(2,1)S(1)}, bf16[3072,1,384]{2,0,1:T(8,128)(2,1)}, u32[]{:S(2)}) copy-start(bf16[3072,1,384]{2,0,1:T(8,128)(2,1)} %param.11) | copy-start | bytes 7077892
  6.5 148.9 %all-gather.5.cloned.1.call-start = ((), (), s32[]{:S(2)}) async-start(), calls=%async_computation.1 | async-start | bytes 13369344 | tf_op jit(solution)/shard_map/all_gather | solution.py:31
  7.3 521.6 %all-gather.7.cloned.1.call-start = ((), (), s32[]{:S(2)}) async-start(), calls=%async_computation.2 | async-start | bytes 17825792 | tf_op jit(solution)/shard_map/all_gather | solution.py:49
  8.0 158.2 %copy-start.2 = (bf16[1,3072,32]{1,2,0:T(8,128)(2,1)S(1)}, bf16[1,3072,32]{1,2,0:T(8,128)(2,1)}, u32[]{:S(2)}) copy-start(bf16[1,3072,32]{1,2,0:T(8,128)(2,1)} %param.13) | copy-start | bytes 589828
  8.0 158.2 %copy-start.3 = (bf16[1,32,1,384]{3,1,2,0:T(8,128)(2,1)S(1)}, bf16[1,32,1,384]{3,1,2,0:T(8,128)(2,1)}, u32[]{:S(2)}) copy-start(bf16[1,32,1,384]{3,1,2,0:T(8,128)(2,1)} %param.14) | copy-start | bytes 73732
  166.2 13.4 %copy-start.5 = (s32[16]{0:T(128)S(1)}, s32[16]{0:T(128)}, u32[]{:S(2)}) copy-start(s32[16]{0:T(128)} %param.17) | copy-start | bytes 196
  166.2 16.1 %copy-start.6 = (s32[4]{0:T(128)S(1)}, s32[4]{0:T(128)}, u32[]{:S(2)}) copy-start(s32[4]{0:T(128)} %param.16) | copy-start | bytes 52
  166.2 18.1 %copy-start.4 = (s32[1,16,32]{2,1,0:T(8,128)S(1)}, s32[1,16,32]{2,1,0:T(8,128)}, u32[]{:S(2)}) copy-start(s32[1,16,32]{2,1,0:T(8,128)} %param.15) | copy-start | bytes 6148
  177.3 355.6 %slice-start = ((bf16[2048,1,384]{2,0,1:T(8,128)(2,1)}), bf16[2048,1,128]{2,0,1:T(8,128)(2,1)S(1)}, s32[]{:S(2)}) async-start(bf16[2048,1,384]{2,0,1:T(8,128)(2,1)} %fusion.16), calls=%async_computation.3 | async-start | bytes 1048576 | tf_op jit(solution)/shard_map/slice | solution.py:45
  539.2 2.5 copy-start.1
  549.4 2.5 copy-start.1
  559.5 2.5 copy-start.1
  569.7 2.5 copy-start.1
Sparse Core Ops, SparseCore 0:
  10.1 145.2 all-gather.4
  179.7 349.1 all-gather.6
where the time goes:
time: 606 us; the launch traced here: 605 us
  waiting for transfers between devices  492 us (81%)
  matrix products  37.7 us (6%)
  blocking collectives  23.1 us (4%)
  other arithmetic  22.5 us (4%)
  between operations  17.5 us (3%)
  local copies, waits for them, and re-layouts  9.18 us (2%)
    all_gather x1, waiting for transfers between devices, on_device(): collected = lax.all_gather(own_pairs[None], 'req', axis=0, tiled=True)  344 us
    all_gather x1, waiting for transfers between devices, on_device(): token_rows = lax.all_gather(own_tokens, 'patch', axis=0, tiled=True)  147 us
    all_to_all x1, blocking collectives, on_device(): lax.all_to_all(shortened(mixed), 'patch', split_axis=0, concat_axis=1, ti...  23.1 us
  transfers between devices with their start and end apart: 2, of which 2 were waited for; matrix products, arithmetic and copies ran while one was open for 0% of the time, Pallas kernels for 0%

commit v1 on v0

v1 whole, which is shorter than its diff:
```python
import functools, math
import jax, jax.numpy as jnp
from jax import lax
from jax.experimental import pallas as pl
from jax.experimental.pallas import tpu as pltpu
from jax.sharding import PartitionSpec as P

MESH = pl.DeviceIdType.MESH
CW, CCW = 0, 1
PIECES = 4
HALVES = ((0, 1), (2, 3))


def place():
    r, p = lax.axis_index("req"), lax.axis_index("patch")
    return lax.div(r, 4), lax.rem(r, 4), lax.div(p, 8), lax.rem(lax.div(p, 2), 4), lax.rem(p, 2)


def at(x, z, y, c):
    z = lax.rem(z, 8)
    return (lax.rem(x, 4) * 4 + lax.rem(z, 4), lax.div(z, 4) * 8 + lax.rem(y, 4) * 2 + c)


def token_kernel(tok, w, down, up, bias, q_out, kv_out, held, relay, own_sem,
                 z1s, z1r, z2s, z2r, ys, yr, ss, sr):
    x, zl, zh, y, c = place()
    z = zh * 4 + zl
    rows = tok.shape[0]
    step = rows // PIECES
    other = 1 - c

    def shard(f, dy, cc):
        half = zh if f == 0 else 1 - zh
        return half * 8 + lax.rem(y + dy, 4) * 2 + cc

    sibling = at(x, z, y, other)
    ring = (at(x, z, y + 1, c), at(x, z, y + 3, c))
    zring = (at(x, z + 2, y, c), at(x, z + 6, y, c))

    barrier = pltpu.get_barrier_semaphore()
    for who in (sibling, *ring, *zring):
        pl.semaphore_signal(barrier, inc=1, device_id=who, device_id_type=MESH)
    pl.semaphore_wait(barrier, 5)

    def span(k):
        return pl.ds(k * step, step)

    def remote(src, dst, send, recv, who):
        return pltpu.make_async_remote_copy(
            src_ref=src, dst_ref=dst, send_sem=send, recv_sem=recv, device_id=who, device_id_type=MESH)

    started = []

    def go(copy):
        copy.start()
        started.append(copy)

    def source(f, k):
        return tok.at[span(k)] if f == 0 else held.at[shard(1, 0, c), span(k)]

    def y_copy(f, way, j):
        if j < 4:
            p, k, src = shard(f, 0, c), j, source(f, j)
        else:
            k = HALVES[way][j - 4]
            p = shard(f, 3 if way == CW else 1, c)
            src = held.at[p, span(k)]
        return remote(src, held.at[p, span(k)], ys.at[f, way, j], yr.at[f, way, j], ring[way])

    def y_arrived(f, way, j):
        if j < 4:
            p, k = shard(f, 3 if way == CW else 1, c), j
        else:
            p, k = shard(f, 2, c), HALVES[way][j - 4]
        piece = held.at[p, span(k)]
        remote(piece, piece, ys.at[f, way, j], yr.at[f, way, j], ring[way]).wait_recv()

    def s_copy(f, dy, k):
        src = tok.at[span(k)] if (f == 0 and dy == 0) else held.at[shard(f, dy, c), span(k)]
        return remote(src, held.at[shard(f, dy, c), span(k)], ss.at[f, dy, k], sr.at[f, dy, k], sibling)

    def s_arrived(f, dy, k):
        piece = held.at[shard(f, dy, other), span(k)]
        remote(piece, piece, ss.at[f, dy, k], sr.at[f, dy, k], sibling).wait_recv()

    def z1_copy(k):
        way = 0 if k < 2 else 1
        return remote(tok.at[span(k)], relay.at[k], z1s.at[k], z1r.at[k], zring[way])

    def z2_copy(k):
        way = 0 if k < 2 else 1
        oz = lax.rem(z + (6 if way == 0 else 2), 8)
        p = lax.div(oz, 4) * 8 + y * 2 + c
        return remote(relay.at[k], held.at[p, span(k)], z2s.at[k], z2r.at[k], zring[way])

    def z1_arrived(k):
        remote(relay.at[k], relay.at[k], z1s.at[k], z1r.at[k], sibling).wait_recv()

    def z2_arrived(k):
        piece = held.at[shard(1, 0, c), span(k)]
        remote(piece, piece, z2s.at[k], z2r.at[k], sibling).wait_recv()

    def project(ref, p):
        t = ref[...]
        low = lax.dot_general(t, down[...], (((1,), (1,)), ((), ())), preferred_element_type=jnp.float32)
        acc = jnp.dot(t, w[...], preferred_element_type=jnp.float32)
        acc = acc + jnp.dot(low.astype(jnp.bfloat16), up[...], preferred_element_type=jnp.float32)
        acc = acc + bias[...].astype(jnp.float32)
        here = pl.ds(pl.multiple_of(p * rows, rows), rows)
        q_out[here, :] = (acc[:, :128] * QSCALE).astype(jnp.bfloat16)
        kv_out[here, :] = acc[:, 128:].astype(jnp.bfloat16)

    def project_shard(f, dy, cc):
        p = shard(f, dy, cc)
        project(held.at[p], p)

    def take_y(f, way, j):
        y_arrived(f, way, j)
        if j < 4:
            if j in HALVES[way]:
                go(y_copy(f, way, 4 + HALVES[way].index(j)))
            go(s_copy(f, 3 if way == CW else 1, j))
        else:
            go(s_copy(f, 2, HALVES[way][j - 4]))

    def relay_on(k):
        z1_arrived(k)
        go(z2_copy(k))

    def take_z(k):
        z2_arrived(k)
        go(y_copy(1, CW, k))
        go(y_copy(1, CCW, k))
        go(s_copy(1, 0, k))

    def sib_ready(f, dy):
        for k in range(PIECES):
            s_arrived(f, dy, k)
        project_shard(f, dy, other)

    for k in (0, 2, 1, 3):
        go(z1_copy(k))
    for j in range(4):
        go(y_copy(0, CW, j))
        go(y_copy(0, CCW, (2, 3, 0, 1)[j]))
    for k in range(PIECES):
        go(s_copy(0, 0, k))

    project(tok, shard(0, 0, c))
    take_y(0, CW, 0)
    take_y(0, CCW, 2)
    sib_ready(0, 0)
    relay_on(0)
    relay_on(2)
    take_y(0, CW, 1)
    take_y(0, CCW, 3)
    take_y(0, CW, 2)
    take_y(0, CCW, 0)
    relay_on(1)
    relay_on(3)
    take_y(0, CW, 3)
    take_y(0, CCW, 1)
    project_shard(0, 3, c)
    project_shard(0, 1, c)
    take_z(0)
    take_z(2)
    sib_ready(0, 3)
    sib_ready(0, 1)
    take_y(0, CW, 4)
    take_y(0, CCW, 4)
    take_y(0, CW, 5)
    take_y(0, CCW, 5)
    take_y(1, CW, 0)
    take_y(1, CCW, 2)
    project_shard(0, 2, c)
    take_z(1)
    take_z(3)
    project_shard(1, 0, c)
    take_y(1, CW, 2)
    take_y(1, CCW, 0)
    sib_ready(0, 2)
    sib_ready(1, 0)
    take_y(1, CW, 1)
    take_y(1, CCW, 3)
    take_y(1, CW, 4)
    take_y(1, CCW, 4)
    take_y(1, CW, 3)
    take_y(1, CCW, 1)
    project_shard(1, 3, c)
    project_shard(1, 1, c)
    take_y(1, CW, 5)
    take_y(1, CCW, 5)
    sib_ready(1, 3)
    sib_ready(1, 1)
    project_shard(1, 2, c)
    sib_ready(1, 2)
    for copy in started:
        copy.wait_send()


QSCALE = math.log2(math.e) / math.sqrt(128)


def gather_project(tok, w, down, up, bias):
    rows, width = tok.shape
    dma = pltpu.SemaphoreType.DMA
    vmem = pl.BlockSpec(memory_space=pltpu.VMEM)
    return pl.pallas_call(
        token_kernel,
        out_shape=(jax.ShapeDtypeStruct((16 * rows, 128), jnp.bfloat16),
                   jax.ShapeDtypeStruct((16 * rows, 256), jnp.bfloat16)),
        in_specs=[vmem] * 5,
        out_specs=(vmem, vmem),
        scratch_shapes=[
            pltpu.VMEM((16, rows, width), jnp.bfloat16),
            pltpu.VMEM((PIECES, rows // PIECES, width), jnp.bfloat16),
            dma,
            dma((4,)), dma((4,)), dma((4,)), dma((4,)),
            dma((2, 2, 6)), dma((2, 2, 6)),
            dma((2, 4, 4)), dma((2, 4, 4)),
        ],
        compiler_params=pltpu.CompilerParams(
            collective_id=0, has_side_effects=True, vmem_limit_bytes=48 * 2**20),
        name="tokens_to_projection",
    )(tok, w, down, up, bias)


CHUNKS = 8


def pick(values, index):
    out = values[0]
    for n in range(1, len(values)):
        out = jnp.where(index == n, values[n], out)
    return out


def exchange_kernel(info, kv, out, xin, rs, rr, ls, lr, xout,
                    x1s, x1r, rsend, rrecv, lsend, lrecv, x2s, x2r):
    x, zl, zh, y, c = place()
    z = zh * 4 + zl
    length = kv.shape[0]
    part = length // (4 * CHUNKS)
    xs = [at(x + d, z, y, c) for d in range(4)]
    right, left = at(x, zh * 4 + lax.rem(zl + 1, 4), y, c), at(x, zh * 4 + lax.rem(zl + 3, 4), y, c)

    barrier = pltpu.get_barrier_semaphore()
    for who in (*xs[1:], right, left):
        pl.semaphore_signal(barrier, inc=1, device_id=who, device_id_type=MESH)
    pl.semaphore_wait(barrier, 5)

    def remote(src, dst, send, recv, who):
        return pltpu.make_async_remote_copy(
            src_ref=src, dst_ref=dst, send_sem=send, recv_sem=recv, device_id=who, device_id_type=MESH)

    def rows(ch, q):
        return pl.ds(pl.multiple_of((ch * 4 + q) * part, part), part)

    def x1_copy(ch, d):
        q = lax.rem(x + d, 4)
        return remote(kv.at[rows(ch, q)], xin.at[ch, x], x1s.at[ch, d], x1r.at[ch, 4 - d], xs[d])

    def x1_arrived(ch, d):
        piece = xin.at[ch, lax.rem(x + d, 4)]
        return remote(piece, piece, x1s.at[ch, d], x1r.at[ch, d], xs[d])

    def x2_copy(ch, d):
        return remote(xout.at[ch, d], out.at[rows(ch, x)], x2s.at[ch, d], x2r.at[ch, 4 - d], xs[d])

    def x2_arrived(ch, d):
        piece = out.at[rows(ch, lax.rem(x + d, 4))]
        return remote(piece, piece, x2s.at[ch, d], x2r.at[ch, d], xs[d])

    def r_copy(ch):
        return remote(rs.at[ch], rr.at[ch], rsend.at[ch], rrecv.at[ch], right)

    def l_copy(ch):
        return remote(ls.at[ch], lr.at[ch], lsend.at[ch], lrecv.at[ch], left)

    def begin(ch, carry):
        for d in (2, 1, 3):
            x1_copy(ch, d).start()
        xin[ch, x] = kv[rows(ch, x), :]
        return carry

    lax.fori_loop(0, CHUNKS, begin, 0)

    def mine(ch, slot):
        held = [xin[ch, n] for n in range(4)]
        return pick(held, info[0, slot])

    def flow(ch, incoming, sendbuf, copy, has_in, has_out):
        @pl.when(has_in)
        def _():
            remote(incoming.at[ch], incoming.at[ch], rsend.at[ch],
                   (rrecv if incoming is rr else lrecv).at[ch], right).wait_recv()

        @pl.when(has_out)
        def _():
            for slot in range(4):
                sendbuf[ch, slot] = jnp.where(info[1, slot] == 1, mine(ch, slot), incoming[ch, slot])
            copy(ch).start()

    def step(t, carry):
        @pl.when(t < CHUNKS)
        def _():
            for d in (1, 3, 2):
                x1_arrived(t, d).wait_recv()

        rc = t - zl
        @pl.when((rc >= 0) & (rc < CHUNKS))
        def _():
            flow(rc, rr, rs, r_copy, zl > 0, zl < 3)

        lc = t - (3 - zl)
        @pl.when((lc >= 0) & (lc < CHUNKS))
        def _():
            flow(lc, lr, ls, l_copy, zl < 3, zl > 0)

        ch = t - 3
        @pl.when(ch >= 0)
        def _():
            final = []
            for slot in range(4):
                far = jnp.where(info[1, slot] == 2, rr[ch, slot], lr[ch, slot])
                final.append(jnp.where(info[1, slot] == 1, mine(ch, slot), far))
            for d in (2, 1, 3):
                xout[ch, d] = pick(final, info[2, d])
                x2_copy(ch, d).start()
            out[rows(ch, x), :] = pick(final, info[2, 0])
        return carry

    lax.fori_loop(0, CHUNKS + 3, step, 0)

    def end(ch, carry):
        for d in (1, 3, 2):
            x2_arrived(ch, d).wait_recv()
            x1_copy(ch, d).wait_send()
            x2_copy(ch, d).wait_send()

        @pl.when(zl < 3)
        def _():
            r_copy(ch).wait_send()

        @pl.when(zl > 0)
        def _():
            l_copy(ch).wait_send()
        return carry

    lax.fori_loop(0, CHUNKS, end, 0)


def routes(references, pairing):
    r = lax.axis_index("req")
    x, zl = r // 4, r % 4
    plane = references % 4
    side = jnp.where(plane == zl, 1, jnp.where(plane < zl, 2, 0))
    slots = jnp.stack([pairing[((x + d) % 4) * 4 + zl] for d in range(4)])
    return jnp.stack([references // 4, side, slots]).astype(jnp.int32)


def exchange(info, kv):
    length, width = kv.shape
    part = length // (4 * CHUNKS)
    dma = pltpu.SemaphoreType.DMA
    vmem = pl.BlockSpec(memory_space=pltpu.VMEM)
    buf = pltpu.VMEM((CHUNKS, 4, part, width), kv.dtype)
    return pl.pallas_call(
        exchange_kernel,
        out_shape=jax.ShapeDtypeStruct((length, width), kv.dtype),
        in_specs=[pl.BlockSpec(memory_space=pltpu.SMEM), vmem],
        out_specs=vmem,
        scratch_shapes=[buf] * 6 + [dma((CHUNKS, 4)), dma((CHUNKS, 4))] + [dma((CHUNKS,))] * 4
        + [dma((CHUNKS, 4)), dma((CHUNKS, 4))],
        compiler_params=pltpu.CompilerParams(
            collective_id=1, has_side_effects=True, vmem_limit_bytes=48 * 2**20),
        name="reference_keys",
    )(info, kv)


TILE = 128
GROUP = 4


def attend_kernel(count, klist, vlist, q, own, theirs, out, keys, values, scores):
    tiles = q.shape[0] // TILE
    length = q.shape[0]

    def rows(t):
        return pl.ds(pl.multiple_of(t * TILE, TILE), TILE)

    def fill(t, carry):
        for ref, base in ((own, 0), (theirs, tiles)):
            keys[rows(base + t), :] = ref[rows(t), :TILE]
            values[rows(base + t), :TILE] = ref[rows(t), TILE:]
            values[rows(base + t), TILE:] = jnp.ones((TILE, TILE), jnp.bfloat16)
        return carry

    lax.fori_loop(0, tiles, fill, 0)
    values[rows(2 * tiles), :] = jnp.zeros((TILE, 2 * TILE), jnp.bfloat16)

    def tile(i, carry):
        qt = q[rows(i), :]
        groups = count[i]

        def first(g, top):
            for n in range(GROUP):
                kt = keys[rows(klist[i, g * GROUP + n]), :]
                s = lax.dot_general(qt, kt, (((1,), (1,)), ((), ())), preferred_element_type=jnp.float32)
                scores[g * GROUP + n] = s
                top = jnp.maximum(top, s)
            return top

        top = lax.fori_loop(0, groups, first, jnp.full((TILE, TILE), -jnp.inf, jnp.float32))
        top = jnp.max(top, axis=1, keepdims=True)

        def second(g, acc):
            for n in range(GROUP):
                p = jnp.exp2(scores[g * GROUP + n] - top).astype(jnp.bfloat16)
                acc = acc + jnp.dot(p, values[rows(vlist[i, g * GROUP + n]), :], preferred_element_type=jnp.float32)
            return acc

        acc = lax.fori_loop(0, groups, second, jnp.zeros((TILE, 2 * TILE), jnp.float32))
        out[rows(i), :] = (acc[:, :TILE] / acc[:, TILE:]).astype(jnp.bfloat16)
        return carry

    lax.fori_loop(0, tiles, tile, 0)


def lists(mask):
    tiles = mask.shape[0]
    i = lax.broadcasted_iota(jnp.int32, (tiles, 2 * tiles), 0)
    j = lax.broadcasted_iota(jnp.int32, (tiles, 2 * tiles), 1)
    allow = ((mask == 1) | (i == j)).astype(jnp.int32)
    total = jnp.sum(allow, axis=1)
    before = jnp.sum(jnp.where(j[0][:, None] < j[0][None, :], allow[:, :, None], 0), axis=1)
    at = (before[:, :, None] == j[0][None, None, :]) & (allow[:, :, None] == 1)
    order = jnp.sum(jnp.where(at, j[:, :, None], 0), axis=1)
    used = j < total[:, None]
    klist = jnp.where(used, order, i)
    vlist = jnp.where(used, order, 2 * tiles)
    return (total + GROUP - 1) // GROUP, klist, vlist


def attend(mask, q, own, theirs):
    length = q.shape[0]
    tiles = length // TILE
    vmem = pl.BlockSpec(memory_space=pltpu.VMEM)
    smem = pl.BlockSpec(memory_space=pltpu.SMEM)
    count, klist, vlist = lists(mask)
    return pl.pallas_call(
        attend_kernel,
        out_shape=jax.ShapeDtypeStruct((length, TILE), jnp.bfloat16),
        in_specs=[smem] * 3 + [vmem] * 3,
        out_specs=vmem,
        scratch_shapes=[
            pltpu.VMEM((2 * length, TILE), jnp.bfloat16),
            pltpu.VMEM((2 * length + TILE, 2 * TILE), jnp.bfloat16),
            pltpu.VMEM((2 * tiles, TILE, TILE), jnp.float32),
        ],
        compiler_params=pltpu.CompilerParams(vmem_limit_bytes=48 * 2**20),
        name="attention",
    )(count, klist, vlist, q, own, theirs)


def on_device(tokens, projection_weight, projection_bias, adapter_down_weight, adapter_up_weight,
              tile_allow_mask, references, pairing):
    q, own = gather_project(tokens[0], projection_weight[:, 0], adapter_down_weight[0].T,
                            adapter_up_weight[0, :, 0], projection_bias)
    theirs = exchange(routes(references, pairing), own)
    mixed = attend(tile_allow_mask[0], q, own, theirs)
    return lax.all_to_all(mixed, "patch", split_axis=0, concat_axis=1, tiled=True)[None]


def solution(mesh):
    in_specs = (
        P("req", "patch", None),
        P(None, "patch", None),
        P("patch", None),
        P("req", None, None),
        P("req", None, "patch", None),
        P("req", None, None),
        P(),
        P(),
    )
    return jax.shard_map(
        on_device, mesh=mesh, in_specs=in_specs, out_specs=P("req", "patch", None), check_vma=False
    )
```

time: 606 us -> 196 us (0.32)
  waiting for transfers between devices: 492 us -> 0 us
  Pallas kernels: 0 us -> 152 us
  matrix products: 37.7 us -> 0 us
  between operations: 17.5 us -> 0.06 us
  other arithmetic: 22.5 us -> 5.3 us
  blocking collectives: 23.1 us -> 30.5 us
    all_gather x2 -> x0, waiting for transfers between devices: 491 us -> none  [the longest x1 344 us: on_device(): collected = lax.all_gather(own_pairs[None], 'req', axis=0, tiled=True)]
    pallas_call x0 -> x3, Pallas kernels: none -> 152 us  [the longest x1 66.1 us: gather_project(): pl.pallas_call(token_kernel, out_shape=(jax.ShapeDtypeStruct((16 * rows,...]
    dot_general x10 -> x0, matrix products: 37.7 us -> none  [the longest x1 11.1 us: on_device(): jnp.einsum('tr,rhe->the', lowrank, local_up_matrix, preferred_element_typ...]
    convert_element_type x4 -> x0, other arithmetic: 9.85 us -> none  [one_block(): probability = (weights / row_total).astype(jnp.bfloat16)]
    reduce_sum x4 -> x3, other arithmetic: 9.22 us -> 1.17 us  [the longest x1 0.81 us: lists(): total = jnp.sum(allow, axis=1)]
    all_to_all x1, blocking collectives: 23.1 us -> 30.5 us  [on_device(): lax.all_to_all(mixed, 'patch', split_axis=0, concat_axis=1, tiled=True)]
  transfers between devices with their start and end apart: 2 -> 0, of which waited for: 2 -> 0; matrix products, arithmetic and copies ran while one was open for 0% -> 0% of each run, Pallas kernels for 0% -> 0%
where the time goes in v1:
time: 196 us; the launch traced here: 195 us
  Pallas kernels  152 us (78%)
  blocking collectives  30.5 us (16%)
  local copies, waits for them, and re-layouts  7.96 us (4%)
  other arithmetic  5.3 us (3%)
    pallas_call x1, Pallas kernels, gather_project(): pl.pallas_call(token_kernel, out_shape=(jax.ShapeDtypeStruct((16 * rows,...  66.1 us
    pallas_call x1, Pallas kernels, exchange(): pl.pallas_call(exchange_kernel, out_shape=jax.ShapeDtypeStruct((length, w...  51.4 us
    pallas_call x1, Pallas kernels, attend(): pl.pallas_call(attend_kernel, out_shape=jax.ShapeDtypeStruct((length, TIL...  34.1 us
    all_to_all x1, blocking collectives, on_device(): lax.all_to_all(mixed, 'patch', split_axis=0, concat_axis=1, tiled=True)  30.5 us
    unnamed x10, local copies, waits for them, and re-layouts  5.13 us

profile of v1, /device:TPU:1, one launch (start us, length us, event | category | flops | bytes accessed | tf_op | source)
XLA Modules:
  0.0 195.3 jit_solution(15712677460592414375)
XLA Ops:
  0.0 0.8 fusion.5
  0.8 0.7 broadcast_compare_fusion.1
  1.5 0.1 broadcast_compare_fusion
  1.6 0.1 select_reduce_fusion.1
  1.8 0.2 select_reduce_fusion
  2.0 0.1 fusion
  2.1 1.5 fusion.6
  3.5 3.2 %fusion.4 = (s32[1,4]{1,0:T(1,128)S(1)}, s32[1,4]{1,0:T(1,128)S(1)}, s32[1,4]{1,0:T(1,128)S(1)}) fusion(s32[4]{0:T(128)} %param.14, s32[]{:T(128)S(6)} %select_n.86, s32[1]{0:T(128)} %get-tuple-element.17, s32[1]{0:T(128)} %get-tuple-element.18, s32[1]{0:T(128)} %get-tuple-element.16, s32[1]{0:T(128)} %get-tuple-element.15), kind=kLoop, calls=%fused_computation.25 | loop fusion | flops 104 | bytes 84 | tf_op jit(solution)/shard_map/stack | solution.py:359
  6.8 0.0 copy-start
  6.8 1.7 copy-done
  8.4 0.0 copy-start.1
  8.4 1.1 copy-done.1
  9.6 0.0 copy-start.2
  9.6 0.9 copy-done.2
  10.5 0.0 copy-start.3
  10.5 0.7 copy-done.3
  11.2 0.0 copy-start.4
  11.2 0.7 copy-done.4
  11.9 66.1 %tokens_to_projection.1 = (bf16[2048,128]{1,0:T(8,128)(2,1)S(1)}, bf16[2048,256]{1,0:T(8,128)(2,1)S(1)}) custom-call(bf16[128,3072]{1,0:T(8,128)(2,1)S(1)} %bitcast.24, bf16[3072,384]{1,0:T(8,128)(2,1)S(1)} %bitcast.22, bf16[32,3072]{1,0:T(8,128)(2,1)S(1)} %bitcast.25, bf16[32,384]{1,0:T(8,128)(2,1)S(1)} %bitcast.26, bf16[1,384]{1,0:T(2,128)(2,1)S(1)} %copy-done.4), custom_call_target="tpu_custom_call" | custom-call | tf_op jit(solution)/shard_map/tokens_to_projection/pallas_call | solution.py:208
  78.0 51.4 %reference_keys.1.theirs = bf16[2048,256]{1,0:T(8,128)(2,1)S(1)} custom-call(s32[3,4]{1,0:T(4,128)S(1)} %pad_add_fusion.info, bf16[2048,256]{1,0:T(8,128)(2,1)S(1)} %get-tuple-element.8.kv.own), custom_call_target="tpu_custom_call" | custom-call | tf_op jit(solution)/shard_map/reference_keys/pallas_call | solution.py:368
  129.4 34.1 %attention.1 = bf16[2048,128]{1,0:T(8,128)(2,1)S(1)} custom-call(s32[16]{0:T(128)S(1)} %and_select_fusion.2.count, s32[16,32]{1,0:T(8,128)S(1)} %get-tuple-element.10.klist, s32[16,32]{1,0:T(8,128)S(1)} %get-tuple-element.9.vlist, bf16[2048,128]{1,0:T(8,128)(2,1)S(1)} %get-tuple-element.7.q, bf16[2048,256]{1,0:T(8,128)(2,1)S(1)} %get-tuple-element.8.kv.own, ...), custom_call_target="tpu_custom_call" | custom-call | tf_op jit(solution)/shard_map/attention/pallas_call | solution.py:451
  163.5 30.5 %all_to_all.16 = bf16[16,128,128]{2,1,0:T(8,128)(2,1)S(1)} all-to-all(bf16[16,128,128]{2,1,0:T(8,128)(2,1)S(1)} %bitcast.23), channel_id=1, replica_groups=mesh['req'=16,'patch'=16] {'patch'}, dimensions={0} | all-to-all | bytes 1048576 | tf_op jit(solution)/shard_map/all_to_all | solution.py:472
  194.0 0.3 copy.10
  194.3 1.0 broadcast_in_dim.49
  (3 shorter events, 0.0 us)
Async XLA Ops:
  6.8 1.7 copy-start
  8.4 1.1 copy-start.1
  9.6 0.9 copy-start.2
  10.5 0.7 copy-start.3
  11.2 0.7 copy-start.4

commit v2 on v0

v2 whole, which is shorter than its diff:
```python
import math

import jax
import jax.numpy as jnp
from jax import lax
from jax.experimental import pallas as pl
from jax.experimental.pallas import tpu as pltpu
from jax.sharding import PartitionSpec as P

MESH = pl.DeviceIdType.MESH
CW, CCW = 0, 1
PIECES = 4
HALVES = ((0, 1), (2, 3))
TILE = 128
HEAD = 128
CHUNKS = 8
QROWS = 512
KROWS = 1024
KSTEP = 256
LOW = -1e30
QSCALE = math.log2(math.e) / math.sqrt(HEAD)
ORDER = ((0, 0), (0, 1), (3, 0), (1, 0), (3, 1), (1, 1), (2, 0), (2, 1))
MIRROR = (0, 1, 3, 2, 5, 4, 6, 7)


def place():
    r, p = lax.axis_index("req"), lax.axis_index("patch")
    return lax.div(r, 4), lax.rem(r, 4), lax.div(p, 8), lax.rem(lax.div(p, 2), 4), lax.rem(p, 2)


def at(x, z, y, c):
    z = lax.rem(z, 8)
    return (lax.rem(x, 4) * 4 + lax.rem(z, 4), lax.div(z, 4) * 8 + lax.rem(y, 4) * 2 + c)


def pick(values, index):
    out = values[0]
    for n in range(1, len(values)):
        out = jnp.where(index == n, values[n], out)
    return out


def block_kernel(references, pairing, mask, bias, tok_hbm, w_hbm, down_hbm, up_hbm, out,
                 held, relay, w, down, up, q, kt, va, kv, refkv, xin, rs, rr, ls, lr, xout,
                 s, top_all, acc_all, mixed,
                 lsem, z1s, z1r, z2s, z2r, ys, yr, ss, sr,
                 x1s, x1r, rsend, rrecv, lsend, lrecv, x2s, x2r, os, orv):
    x, zl, zh, y, c = place()
    z = zh * 4 + zl
    rows = tok_hbm.shape[0]
    step = rows // PIECES
    part = 2 * rows // 4
    other = 1 - c
    me = zh * 8 + y * 2 + c

    def shard(f, dy, cc):
        half = zh if f == 0 else 1 - zh
        return half * 8 + lax.rem(y + dy, 4) * 2 + cc

    def logical(j):
        f, (dy, o) = j // 8, ORDER[j % 8]
        return f, dy, (other if o else c)

    tok = held.at[me]
    local = [
        pltpu.make_async_copy(tok_hbm, tok, lsem.at[0]),
        pltpu.make_async_copy(w_hbm, w, lsem.at[1]),
        pltpu.make_async_copy(down_hbm, down, lsem.at[2]),
        pltpu.make_async_copy(up_hbm, up, lsem.at[3]),
    ]
    for copy in local:
        copy.start()

    sibling = at(x, z, y, other)
    ring = (at(x, z, y + 1, c), at(x, z, y + 3, c))
    zring = (at(x, z + 2, y, c), at(x, z + 6, y, c))
    xs = [at(x + d, z, y, c) for d in range(4)]
    right = at(x, zh * 4 + lax.rem(zl + 1, 4), y, c)
    left = at(x, zh * 4 + lax.rem(zl + 3, 4), y, c)
    owners = []
    for j in range(16):
        f, dy, cc = logical(j)
        owners.append((x * 4 + zl, shard(f, dy, cc)))

    barrier = pltpu.get_barrier_semaphore()
    everyone = (*owners[1:], *zring, *xs[1:], right, left)
    for who in everyone:
        pl.semaphore_signal(barrier, inc=1, device_id=who, device_id_type=MESH)
    pl.semaphore_wait(barrier, len(everyone))

    def remote(src, dst, send, recv, who):
        return pltpu.make_async_remote_copy(
            src_ref=src, dst_ref=dst, send_sem=send, recv_sem=recv, device_id=who, device_id_type=MESH)

    started = []

    def go(copy):
        copy.start()
        started.append(copy)

    def span(k):
        return pl.ds(k * step, step)

    def y_copy(f, way, j):
        if j < 4:
            p, k = shard(f, 0, c), j
        else:
            p, k = shard(f, 3 if way == CW else 1, c), HALVES[way][j - 4]
        piece = held.at[p, span(k)]
        return remote(piece, piece, ys.at[f, way, j], yr.at[f, way, j], ring[way])

    def y_arrived(f, way, j):
        if j < 4:
            p, k = shard(f, 3 if way == CW else 1, c), j
        else:
            p, k = shard(f, 2, c), HALVES[way][j - 4]
        piece = held.at[p, span(k)]
        remote(piece, piece, ys.at[f, way, j], yr.at[f, way, j], ring[way]).wait_recv()

    def s_copy(f, dy, k):
        piece = held.at[shard(f, dy, c), span(k)]
        return remote(piece, piece, ss.at[f, dy, k], sr.at[f, dy, k], sibling)

    def s_arrived(f, dy, k):
        piece = held.at[shard(f, dy, other), span(k)]
        remote(piece, piece, ss.at[f, dy, k], sr.at[f, dy, k], sibling).wait_recv()

    def z1_copy(k):
        return remote(tok.at[span(k)], relay.at[k], z1s.at[k], z1r.at[k], zring[0 if k < 2 else 1])

    def z2_copy(k):
        way = 0 if k < 2 else 1
        oz = lax.rem(z + (6 if way == 0 else 2), 8)
        p = lax.div(oz, 4) * 8 + y * 2 + c
        return remote(relay.at[k], held.at[p, span(k)], z2s.at[k], z2r.at[k], zring[way])

    def take_y(f, way, j):
        y_arrived(f, way, j)
        if j < 4:
            if j in HALVES[way]:
                go(y_copy(f, way, 4 + HALVES[way].index(j)))
            go(s_copy(f, 3 if way == CW else 1, j))
        else:
            go(s_copy(f, 2, HALVES[way][j - 4]))

    def relay_on(k):
        remote(relay.at[k], relay.at[k], z1s.at[k], z1r.at[k], sibling).wait_recv()
        go(z2_copy(k))

    def take_z(k):
        piece = held.at[shard(1, 0, c), span(k)]
        remote(piece, piece, z2s.at[k], z2r.at[k], sibling).wait_recv()
        go(y_copy(1, CW, k))
        go(y_copy(1, CCW, k))
        go(s_copy(1, 0, k))

    def project(j):
        f, dy, cc = logical(j)
        if ORDER[j % 8][1]:
            for k in range(PIECES):
                s_arrived(f, dy, k)
        t = held[shard(f, dy, cc)]
        low = lax.dot_general(t, down[...], (((1,), (1,)), ((), ())), preferred_element_type=jnp.float32)
        acc = jnp.dot(t, w[...], preferred_element_type=jnp.float32)
        acc = acc + jnp.dot(low.astype(jnp.bfloat16), up[...], preferred_element_type=jnp.float32)
        acc = acc + bias[...].astype(jnp.float32)
        here = slice(j * rows, (j + 1) * rows)
        q[here, :HEAD] = (acc[:, :HEAD] * QSCALE).astype(jnp.bfloat16)
        column = lax.broadcasted_iota(jnp.int32, (rows, HEAD), 1)
        q[here, HEAD:] = jnp.where(column == j, 1.0, 0.0).astype(jnp.bfloat16)
        kv[here, :] = acc[:, HEAD:].astype(jnp.bfloat16)
        kt[:HEAD, here] = acc[:, HEAD:2 * HEAD].T.astype(jnp.bfloat16)
        va[here, :HEAD] = acc[:, 2 * HEAD:].astype(jnp.bfloat16)

    def piece_rows(ch, n):
        return pl.ds(pl.multiple_of(ch * (4 * part) + n * part, part), part)

    def x1_copy(ch, d):
        return remote(kv.at[piece_rows(ch, lax.rem(x + d, 4))], xin.at[ch, x], x1s.at[ch, d], x1r.at[ch, 4 - d], xs[d])

    def x2_copy(ch, d):
        return remote(xout.at[ch, d], refkv.at[piece_rows(ch, x)], x2s.at[ch, d], x2r.at[ch, 4 - d], xs[d])

    def r_copy(ch):
        return remote(rs.at[ch], rr.at[ch], rsend.at[ch], rrecv.at[ch], right)

    def l_copy(ch):
        return remote(ls.at[ch], lr.at[ch], lsend.at[ch], lrecv.at[ch], left)

    columns = [lax.div(references[n], 4) for n in range(4)]
    planes = [lax.rem(references[n], 4) for n in range(4)]
    slots = [pairing[lax.rem(x + d, 4) * 4 + zl] for d in range(4)]

    def keys_send(ch):
        for d in (2, 1, 3):
            go(x1_copy(ch, d))
        xin[ch, x] = kv[piece_rows(ch, x), :]

    def mine(ch, slot):
        return pick([xin[ch, n] for n in range(4)], columns[slot])

    def keys_step(t):
        if t < CHUNKS:
            for d in (1, 3, 2):
                piece = xin.at[t, lax.rem(x + d, 4)]
                remote(piece, piece, x1s.at[t, d], x1r.at[t, d], xs[d]).wait_recv()

        rc = t - zl

        @pl.when((rc >= 0) & (rc < CHUNKS))
        def _():
            @pl.when(zl > 0)
            def _():
                remote(rr.at[rc], rr.at[rc], rsend.at[rc], rrecv.at[rc], left).wait_recv()

            @pl.when(zl < 3)
            def _():
                for slot in range(4):
                    rs[rc, slot] = jnp.where(planes[slot] == zl, mine(rc, slot), rr[rc, slot])
                r_copy(rc).start()

        lc = t - (3 - zl)

        @pl.when((lc >= 0) & (lc < CHUNKS))
        def _():
            @pl.when(zl < 3)
            def _():
                remote(lr.at[lc], lr.at[lc], lsend.at[lc], lrecv.at[lc], right).wait_recv()

            @pl.when(zl > 0)
            def _():
                for slot in range(4):
                    ls[lc, slot] = jnp.where(planes[slot] == zl, mine(lc, slot), lr[lc, slot])
                l_copy(lc).start()

        ch = t - 3
        if ch >= 0:
            final = []
            for slot in range(4):
                far = jnp.where(planes[slot] < zl, rr[ch, slot], lr[ch, slot])
                final.append(jnp.where(planes[slot] == zl, mine(ch, slot), far))
            for d in (2, 1, 3):
                xout[ch, d] = pick(final, slots[d])
                go(x2_copy(ch, d))
            refkv[piece_rows(ch, x), :] = pick(final, slots[0])

    def keys_take(ch):
        for d in (1, 3, 2):
            piece = refkv.at[piece_rows(ch, lax.rem(x + d, 4))]
            remote(piece, piece, x2s.at[ch, d], x2r.at[ch, d], xs[d]).wait_recv()
        size = 4 * part
        got = refkv[ch * size:(ch + 1) * size, :]
        base = 16 * rows + ch * size
        kt[:HEAD, base:base + size] = got[:, :HEAD].astype(jnp.float32).T.astype(jnp.bfloat16)
        va[base:base + size, :HEAD] = got[:, HEAD:]

    def unit(b, block, first=False):
        here = pl.ds(pl.multiple_of(b * QROWS, QROWS), QROWS)
        qt = q[here, :]
        top = None
        for n in range(KROWS // KSTEP):
            k0 = block * KROWS + n * KSTEP
            score = jnp.dot(qt, kt[:, k0:k0 + KSTEP], preferred_element_type=jnp.float32)
            s[:, n * KSTEP:(n + 1) * KSTEP] = score
            for m in range(KSTEP // 128):
                piece = score[:, m * 128:(m + 1) * 128]
                top = piece if top is None else jnp.maximum(top, piece)
        top = jnp.max(top, axis=1, keepdims=True)
        acc = None
        if not first:
            old = top_all[here, :1]
            top = jnp.maximum(top, old)
            acc = acc_all[here, :] * jnp.exp2(old - top)
        top_all[here, :] = jnp.broadcast_to(top, (QROWS, 128))
        for n in range(KROWS // KSTEP):
            k0 = block * KROWS + n * KSTEP
            weight = jnp.exp2((s[:, n * KSTEP:(n + 1) * KSTEP] - top).astype(jnp.bfloat16))
            more = jnp.dot(weight, va[k0:k0 + KSTEP, :], preferred_element_type=jnp.float32)
            acc = more if acc is None else acc + more
        return here, acc

    def units(b0, b1, block, first=False):
        def body(b, carry):
            here, acc = unit(b, block, first)
            acc_all[here, :] = acc
            return carry

        lax.fori_loop(b0, b1, body, 0)

    def my_columns():
        return pl.ds(pl.multiple_of(me * HEAD, HEAD), HEAD)

    def o_copy(j):
        place_there = (j // 8) * 8 + MIRROR[j % 8]
        return remote(mixed.at[j], out.at[:, my_columns()], os.at[j], orv.at[place_there], owners[j])

    def finish(b):
        here, acc = unit(b, 3)
        result = (acc[:, :HEAD] / acc[:, HEAD:HEAD + 1]).astype(jnp.bfloat16)
        for n in range(QROWS // TILE):
            j = b * (QROWS // TILE) + n
            if j == 0:
                out[:, my_columns()] = result[:TILE]
            else:
                mixed[j] = result[n * TILE:(n + 1) * TILE]
                go(o_copy(j))

    local[0].wait()
    for k in (0, 2, 1, 3):
        go(z1_copy(k))
    for j in range(4):
        go(y_copy(0, CW, j))
        go(y_copy(0, CCW, (2, 3, 0, 1)[j]))
    for k in range(PIECES):
        go(s_copy(0, 0, k))

    tiles = mask.shape[0]
    tile_row = lax.broadcasted_iota(jnp.int32, (tiles, 2 * tiles), 0)
    tile_col = lax.broadcasted_iota(jnp.int32, (tiles, 2 * tiles), 1)
    allow = jnp.where((mask[...] == 1) | (tile_row == tile_col), 1.0, 0.0).astype(jnp.bfloat16)

    def order_of(tile):
        far = jnp.where(lax.div(tile, 8) == zh, 0, 8)
        dy = lax.rem(lax.rem(lax.div(tile, 2), 4) + 4 - y, 4)
        o = jnp.where(lax.rem(tile, 2) == c, 0, 1)
        near = jnp.where(dy == 0, o, jnp.where(dy == 2, 6 + o, jnp.where(dy == 3, 2, 3) + 2 * o))
        return far + near

    turn = jnp.where(
        order_of(lax.broadcasted_iota(jnp.int32, (tiles, tiles), 1)) == lax.broadcasted_iota(jnp.int32, (tiles, tiles), 0),
        1.0, 0.0).astype(jnp.bfloat16)
    turned = jnp.dot(turn, allow, preferred_element_type=jnp.float32).astype(jnp.bfloat16)
    spread_shape = (tiles, tiles * TILE)
    spread = jnp.where(
        order_of(lax.broadcasted_iota(jnp.int32, spread_shape, 0)) == lax.div(lax.broadcasted_iota(jnp.int32, spread_shape, 1), TILE),
        1.0, 0.0).astype(jnp.bfloat16)
    for side in range(2):
        wide = jnp.dot(turned[:, side * tiles:(side + 1) * tiles], spread, preferred_element_type=jnp.float32)
        kt[HEAD:HEAD + tiles, side * tiles * TILE:(side + 1) * tiles * TILE] = jnp.where(wide > 0.5, 0.0, LOW).astype(jnp.bfloat16)
    kt[HEAD + tiles:, :] = jnp.zeros((HEAD - tiles, 2 * tiles * TILE), jnp.bfloat16)
    va[:, HEAD:] = jnp.ones((2 * tiles * TILE, HEAD), jnp.bfloat16)

    for copy in local[1:]:
        copy.wait()
    project(0)
    take_y(0, CW, 0)
    take_y(0, CCW, 2)
    project(1)
    keys_send(0)
    relay_on(0)
    relay_on(2)
    take_y(0, CW, 1)
    take_y(0, CCW, 3)
    take_y(0, CW, 2)
    take_y(0, CCW, 0)
    relay_on(1)
    relay_on(3)
    take_y(0, CW, 3)
    take_y(0, CCW, 1)
    project(2)
    project(3)
    keys_send(1)
    take_z(0)
    take_z(2)
    keys_step(0)
    project(4)
    project(5)
    keys_send(2)
    take_y(0, CW, 4)
    take_y(0, CCW, 4)
    take_y(0, CW, 5)
    take_y(0, CCW, 5)
    take_y(1, CW, 0)
    take_y(1, CCW, 2)
    keys_step(1)
    project(6)
    take_z(1)
    take_z(3)
    project(8)
    take_y(1, CW, 2)
    take_y(1, CCW, 0)
    project(7)
    keys_send(3)
    keys_step(2)
    project(9)
    keys_send(4)
    take_y(1, CW, 1)
    take_y(1, CCW, 3)
    keys_step(3)
    take_y(1, CW, 4)
    take_y(1, CCW, 4)
    units(0, 2, 0, True)
    take_y(1, CW, 3)
    take_y(1, CCW, 1)
    keys_step(4)
    project(10)
    project(11)
    keys_send(5)
    take_y(1, CW, 5)
    take_y(1, CCW, 5)
    keys_step(5)
    project(12)
    project(13)
    keys_send(6)
    project(14)
    project(15)
    keys_send(7)
    keys_step(6)
    units(2, 4, 0, True)
    keys_step(7)
    for ch in range(4):
        keys_take(ch)
    units(0, 2, 1)
    keys_step(8)
    units(2, 4, 1)
    keys_step(9)
    units(0, 2, 2)
    keys_step(10)
    units(2, 4, 2)
    for ch in range(4, 8):
        keys_take(ch)
    for b in (2, 3, 0, 1):
        finish(b)
    for j in range(1, 16):
        f, dy, cc = logical(j)
        there = out.at[:, pl.ds(pl.multiple_of(shard(f, dy, cc) * HEAD, HEAD), HEAD)]
        remote(there, there, os.at[j], orv.at[j], owners[j]).wait_recv()
    for copy in started:
        copy.wait_send()

    @pl.when(zl < 3)
    def _():
        for ch in range(CHUNKS):
            r_copy(ch).wait_send()

    @pl.when(zl > 0)
    def _():
        for ch in range(CHUNKS):
            l_copy(ch).wait_send()


def whole_block(references, pairing, mask, bias, tok, w, down, up):
    rows, width = tok.shape
    length = 16 * rows
    dma = pltpu.SemaphoreType.DMA
    vmem = pl.BlockSpec(memory_space=pltpu.VMEM)
    smem = pl.BlockSpec(memory_space=pltpu.SMEM)
    anywhere = pl.BlockSpec(memory_space=pl.ANY)
    half = jnp.bfloat16
    pieces = pltpu.VMEM((CHUNKS, 4, rows // 2, 2 * HEAD), half)
    return pl.pallas_call(
        block_kernel,
        out_shape=jax.ShapeDtypeStruct((rows, 16 * HEAD), half),
        in_specs=[smem, smem, vmem, vmem] + [anywhere] * 4,
        out_specs=vmem,
        scratch_shapes=[
            pltpu.VMEM((16, rows, width), half),
            pltpu.VMEM((PIECES, rows // PIECES, width), half),
            pltpu.VMEM(w.shape, half),
            pltpu.VMEM(down.shape, half),
            pltpu.VMEM(up.shape, half),
            pltpu.VMEM((length, 2 * HEAD), half),
            pltpu.VMEM((2 * HEAD, 2 * length), half),
            pltpu.VMEM((2 * length, 2 * HEAD), half),
            pltpu.VMEM((length, 2 * HEAD), half),
            pltpu.VMEM((length, 2 * HEAD), half),
            pieces, pieces, pieces, pieces, pieces, pieces,
            pltpu.VMEM((QROWS, KROWS), jnp.float32),
            pltpu.VMEM((length, 128), jnp.float32),
            pltpu.VMEM((length, 2 * HEAD), jnp.float32),
            pltpu.VMEM((16, rows, HEAD), half),
            dma((4,)),
            dma((4,)), dma((4,)), dma((4,)), dma((4,)),
            dma((2, 2, 6)), dma((2, 2, 6)),
            dma((2, 4, 4)), dma((2, 4, 4)),
            dma((CHUNKS, 4)), dma((CHUNKS, 4)),
            dma((CHUNKS,)), dma((CHUNKS,)), dma((CHUNKS,)), dma((CHUNKS,)),
            dma((CHUNKS, 4)), dma((CHUNKS, 4)),
            dma((16,)), dma((16,)),
        ],
        compiler_params=pltpu.CompilerParams(
            collective_id=0, has_side_effects=True, vmem_limit_bytes=56 * 2**20),
        name="attention_block",
    )(references, pairing, mask, bias, tok, w, down, up)


def on_device(tokens, projection_weight, projection_bias, adapter_down_weight, adapter_up_weight,
              tile_allow_mask, references, pairing):
    return whole_block(references, pairing, tile_allow_mask[0], projection_bias, tokens[0],
                       projection_weight[:, 0], adapter_down_weight[0].T, adapter_up_weight[0, :, 0])[None]


def solution(mesh):
    in_specs = (
        P("req", "patch", None),
        P(None, "patch", None),
        P("patch", None),
        P("req", None, None),
        P("req", None, "patch", None),
        P("req", None, None),
        P(),
        P(),
    )
    return jax.shard_map(
        on_device, mesh=mesh, in_specs=in_specs, out_specs=P("req", "patch", None), check_vma=False
    )
```

time: 606 us -> 127 us (0.21)
  waiting for transfers between devices: 492 us -> 0 us
  Pallas kernels: 0 us -> 125 us
  matrix products: 37.7 us -> 0 us
  blocking collectives: 23.1 us -> 0 us
  other arithmetic: 22.5 us -> 0 us
  between operations: 17.5 us -> 0.01 us
  local copies, waits for them, and re-layouts: 9.18 us -> 1.88 us
    all_gather x2 -> x0, waiting for transfers between devices: 491 us -> none  [the longest x1 344 us: on_device(): collected = lax.all_gather(own_pairs[None], 'req', axis=0, tiled=True)]
    pallas_call x0 -> x1, Pallas kernels: none -> 125 us  [whole_block(): pl.pallas_call(block_kernel, out_shape=jax.ShapeDtypeStruct((rows, 16 * H...]
    dot_general x10 -> x0, matrix products: 37.7 us -> none  [the longest x1 11.1 us: on_device(): jnp.einsum('tr,rhe->the', lowrank, local_up_matrix, preferred_element_typ...]
    all_to_all x1 -> x0, blocking collectives: 23.1 us -> none  [on_device(): lax.all_to_all(shortened(mixed), 'patch', split_axis=0, concat_axis=1, ti...]
    convert_element_type x4 -> x0, other arithmetic: 9.85 us -> none  [one_block(): probability = (weights / row_total).astype(jnp.bfloat16)]
    reduce_sum x4 -> x0, other arithmetic: 9.22 us -> none  [one_block(): row_total = jnp.sum(weights, axis=-1, keepdims=True)]
  transfers between devices with their start and end apart: 2 -> 0, of which waited for: 2 -> 0; matrix products, arithmetic and copies ran while one was open for 0% -> 0% of each run, Pallas kernels for 0% -> 0%
where the time goes in v2:
time: 127 us
  Pallas kernels  125 us (98%)
  local copies, waits for them, and re-layouts  1.88 us (1%)
    pallas_call x1, Pallas kernels, whole_block(): pl.pallas_call(block_kernel, out_shape=jax.ShapeDtypeStruct((rows, 16 * H...  125 us

profile of v2, /device:TPU:1, one launch (start us, length us, event | category | flops | bytes accessed | tf_op | source)
XLA Modules:
  0.0 126.8 jit_solution(14728123560716980475)
XLA Ops:
  0.0 124.9 %attention_block.1 = bf16[128,2048]{1,0:T(8,128)(2,1)} custom-call(s32[4]{0:T(128)} %references.1, s32[16]{0:T(128)} %pairing.1, s32[16,32]{1,0:T(8,128)} %bitcast.13, bf16[1,384]{1,0:T(2,128)(2,1)} %bias.1, bf16[128,3072]{1,0:T(8,128)(2,1)} %bitcast.10, bf16[3072,384]{1,0:T(8,128)(2,1)} %bitcast.8, bf16[32,3072]{1,0:T(8,128)(2,1)} %bitcast.11, ...), custom_call_target="tpu_custom_call" | custom-call | tf_op jit(solution)/shard_map/attention_block/pallas_call | solution.py:451
  124.9 1.9 %copy.10 = bf16[1,128,2048]{2,1,0:T(8,128)(2,1)} copy(bf16[1,128,2048]{2,1,0:T(8,128)(2,1)} %bitcast.9) | data formatting | bytes 1048576

commit v3 on v2

--- a/solution.py
+++ b/solution.py
@@ -13,11 +13,15 @@
 HALVES = ((0, 1), (2, 3))
 TILE = 128
 HEAD = 128
-CHUNKS = 8
+SIZES = (2, 2, 2, 2, 2, 2, 2, 1, 1)
+STARTS = tuple(sum(SIZES[:n]) for n in range(len(SIZES)))
+CHUNKS = len(SIZES)
+LAG = 2
 QROWS = 512
 KROWS = 1024
 KSTEP = 256
 LOW = -1e30
+OWN0, OWN1, REF0, REF1, LAST = (0, 1024), (1024, 2048), (2048, 3072), (3072, 3840), (3840, 4096)
 QSCALE = math.log2(math.e) / math.sqrt(HEAD)
 ORDER = ((0, 0), (0, 1), (3, 0), (1, 0), (3, 1), (1, 1), (2, 0), (2, 1))
 MIRROR = (0, 1, 3, 2, 5, 4, 6, 7)
@@ -41,7 +45,7 @@
 
 
 def block_kernel(references, pairing, mask, bias, tok_hbm, w_hbm, down_hbm, up_hbm, out,
-                 held, relay, w, down, up, q, kt, va, kv, refkv, xin, rs, rr, ls, lr, xout,
+                 held, relay, w, down, up, q, kt, va, kv, refkv, xin, chosen, rs, rr, ls, lr, xout,
                  s, top_all, acc_all, mixed,
                  lsem, z1s, z1r, z2s, z2r, ys, yr, ss, sr,
                  x1s, x1r, rsend, rrecv, lsend, lrecv, x2s, x2r, os, orv):
@@ -49,7 +53,7 @@
     z = zh * 4 + zl
     rows = tok_hbm.shape[0]
     step = rows // PIECES
-    part = 2 * rows // 4
+    quarter = rows // 4
     other = 1 - c
     me = zh * 8 + y * 2 + c
 
@@ -83,7 +87,7 @@
         owners.append((x * 4 + zl, shard(f, dy, cc)))
 
     barrier = pltpu.get_barrier_semaphore()
-    everyone = (*owners[1:], *zring, *xs[1:], right, left)
+    everyone = (sibling, *ring, *zring, *xs[1:], right, left)
     for who in everyone:
         pl.semaphore_signal(barrier, inc=1, device_id=who, device_id_type=MESH)
     pl.semaphore_wait(barrier, len(everyone))
@@ -172,20 +176,28 @@
         kt[:HEAD, here] = acc[:, HEAD:2 * HEAD].T.astype(jnp.bfloat16)
         va[here, :HEAD] = acc[:, 2 * HEAD:].astype(jnp.bfloat16)
 
+    def size(ch):
+        return SIZES[ch] * quarter
+
     def piece_rows(ch, n):
-        return pl.ds(pl.multiple_of(ch * (4 * part) + n * part, part), part)
+        return pl.ds(pl.multiple_of(STARTS[ch] * rows + n * size(ch), quarter), size(ch))
+
+    def first(ch):
+        return pl.ds(0, size(ch))
 
     def x1_copy(ch, d):
-        return remote(kv.at[piece_rows(ch, lax.rem(x + d, 4))], xin.at[ch, x], x1s.at[ch, d], x1r.at[ch, 4 - d], xs[d])
+        return remote(kv.at[piece_rows(ch, lax.rem(x + d, 4))], xin.at[ch, x, first(ch)],
+                      x1s.at[ch, d], x1r.at[ch, 4 - d], xs[d])
 
     def x2_copy(ch, d):
-        return remote(xout.at[ch, d], refkv.at[piece_rows(ch, x)], x2s.at[ch, d], x2r.at[ch, 4 - d], xs[d])
+        return remote(xout.at[ch, d, first(ch)], refkv.at[piece_rows(ch, x)],
+                      x2s.at[ch, d], x2r.at[ch, 4 - d], xs[d])
 
     def r_copy(ch):
-        return remote(rs.at[ch], rr.at[ch], rsend.at[ch], rrecv.at[ch], right)
+        return remote(rs.at[ch, :, first(ch)], rr.at[ch, :, first(ch)], rsend.at[ch], rrecv.at[ch], right)
 
     def l_copy(ch):
-        return remote(ls.at[ch], lr.at[ch], lsend.at[ch], lrecv.at[ch], left)
+        return remote(ls.at[ch, :, first(ch)], lr.at[ch, :, first(ch)], lsend.at[ch], lrecv.at[ch], left)
 
     columns = [lax.div(references[n], 4) for n in range(4)]
     planes = [lax.rem(references[n], 4) for n in range(4)]
@@ -194,53 +206,63 @@
     def keys_send(ch):
         for d in (2, 1, 3):
             go(x1_copy(ch, d))
-        xin[ch, x] = kv[piece_rows(ch, x), :]
-
-    def mine(ch, slot):
-        return pick([xin[ch, n] for n in range(4)], columns[slot])
+        xin[ch, x, first(ch)] = kv[piece_rows(ch, x), :]
+
+    def is_mine(slot):
+        return planes[slot] == zl
+
+    def flow(ch, copy, incoming, outgoing, source, sink):
+        if source:
+            piece = incoming.at[ch, :, first(ch)]
+            if incoming is rr:
+                remote(piece, piece, rsend.at[ch], rrecv.at[ch], left).wait_recv()
+            else:
+                remote(piece, piece, lsend.at[ch], lrecv.at[ch], right).wait_recv()
+        if sink:
+            for slot in range(4):
+                value = chosen[ch, slot, first(ch)]
+                if source:
+                    value = jnp.where(is_mine(slot), value, incoming[ch, slot, first(ch)])
+                outgoing[ch, slot, first(ch)] = value
+            copy(ch).start()
 
     def keys_step(t):
         if t < CHUNKS:
             for d in (1, 3, 2):
-                piece = xin.at[t, lax.rem(x + d, 4)]
+                piece = xin.at[t, lax.rem(x + d, 4), first(t)]
                 remote(piece, piece, x1s.at[t, d], x1r.at[t, d], xs[d]).wait_recv()
-
-        rc = t - zl
-
-        @pl.when((rc >= 0) & (rc < CHUNKS))
-        def _():
-            @pl.when(zl > 0)
+            here = [xin[t, n, first(t)] for n in range(4)]
+            for slot in range(4):
+                chosen[t, slot, first(t)] = pick(here, columns[slot])
+
+        for line in range(4):
+            rc, lc = t - LAG * line, t - LAG * (3 - line)
+
+            @pl.when(zl == line)
             def _():
-                remote(rr.at[rc], rr.at[rc], rsend.at[rc], rrecv.at[rc], left).wait_recv()
-
-            @pl.when(zl < 3)
-            def _():
-                for slot in range(4):
-                    rs[rc, slot] = jnp.where(planes[slot] == zl, mine(rc, slot), rr[rc, slot])
-                r_copy(rc).start()
-
-        lc = t - (3 - zl)
-
-        @pl.when((lc >= 0) & (lc < CHUNKS))
-        def _():
-            @pl.when(zl < 3)
-            def _():
-                remote(lr.at[lc], lr.at[lc], lsend.at[lc], lrecv.at[lc], right).wait_recv()
-
-            @pl.when(zl > 0)
-            def _():
-                for slot in range(4):
-                    ls[lc, slot] = jnp.where(planes[slot] == zl, mine(lc, slot), lr[lc, slot])
-                l_copy(lc).start()
-
-        ch = t - 3
-        if ch >= 0:
+                def rightward():
+                    if 0 <= rc < CHUNKS:
+                        flow(rc, r_copy, rr, rs, line > 0, line < 3)
+
+                def leftward():
+                    if 0 <= lc < CHUNKS:
+                        flow(lc, l_copy, lr, ls, line < 3, line > 0)
+
+                if line < 2:
+                    rightward()
+                    leftward()
+                else:
+                    leftward()
+                    rightward()
+
+        ch = t - 3 * LAG
+        if 0 <= ch < CHUNKS:
             final = []
             for slot in range(4):
-                far = jnp.where(planes[slot] < zl, rr[ch, slot], lr[ch, slot])
-                final.append(jnp.where(planes[slot] == zl, mine(ch, slot), far))
+                far = jnp.where(planes[slot] < zl, rr[ch, slot, first(ch)], lr[ch, slot, first(ch)])
+                final.append(jnp.where(is_mine(slot), chosen[ch, slot, first(ch)], far))
             for d in (2, 1, 3):
-                xout[ch, d] = pick(final, slots[d])
+                xout[ch, d, first(ch)] = pick(final, slots[d])
                 go(x2_copy(ch, d))
             refkv[piece_rows(ch, x), :] = pick(final, slots[0])
 
@@ -248,44 +270,53 @@
         for d in (1, 3, 2):
             piece = refkv.at[piece_rows(ch, lax.rem(x + d, 4))]
             remote(piece, piece, x2s.at[ch, d], x2r.at[ch, d], xs[d]).wait_recv()
-        size = 4 * part
-        got = refkv[ch * size:(ch + 1) * size, :]
-        base = 16 * rows + ch * size
-        kt[:HEAD, base:base + size] = got[:, :HEAD].astype(jnp.float32).T.astype(jnp.bfloat16)
-        va[base:base + size, :HEAD] = got[:, HEAD:]
-
-    def unit(b, block, first=False):
-        here = pl.ds(pl.multiple_of(b * QROWS, QROWS), QROWS)
-        qt = q[here, :]
+        count = SIZES[ch] * rows
+        got = refkv[STARTS[ch] * rows:STARTS[ch] * rows + count, :]
+        base = (16 + STARTS[ch]) * rows
+        kt[:HEAD, base:base + count] = got[:, :HEAD].astype(jnp.float32).T.astype(jnp.bfloat16)
+        va[base:base + count, :HEAD] = got[:, HEAD:]
+
+    def block(b):
+        return slice(b * QROWS, (b + 1) * QROWS)
+
+    def scores(b, keys, slot):
+        k0, k1 = keys
+        qt = q[block(b), :]
         top = None
-        for n in range(KROWS // KSTEP):
-            k0 = block * KROWS + n * KSTEP
-            score = jnp.dot(qt, kt[:, k0:k0 + KSTEP], preferred_element_type=jnp.float32)
-            s[:, n * KSTEP:(n + 1) * KSTEP] = score
+        for k in range(k0, k1, KSTEP):
+            score = jnp.dot(qt, kt[:, k:k + KSTEP], preferred_element_type=jnp.float32)
+            s[slot, :, k - k0:k - k0 + KSTEP] = score
             for m in range(KSTEP // 128):
                 piece = score[:, m * 128:(m + 1) * 128]
                 top = piece if top is None else jnp.maximum(top, piece)
-        top = jnp.max(top, axis=1, keepdims=True)
+        return jnp.broadcast_to(jnp.max(top, axis=1, keepdims=True), (QROWS, 128))
+
+    def mix(b, keys, slot, top, fresh):
+        k0, k1 = keys
         acc = None
-        if not first:
-            old = top_all[here, :1]
+        if not fresh:
+            old = top_all[block(b), :]
             top = jnp.maximum(top, old)
-            acc = acc_all[here, :] * jnp.exp2(old - top)
-        top_all[here, :] = jnp.broadcast_to(top, (QROWS, 128))
-        for n in range(KROWS // KSTEP):
-            k0 = block * KROWS + n * KSTEP
-            weight = jnp.exp2((s[:, n * KSTEP:(n + 1) * KSTEP] - top).astype(jnp.bfloat16))
-            more = jnp.dot(weight, va[k0:k0 + KSTEP, :], preferred_element_type=jnp.float32)
+            shrink = jnp.exp2(old - top)
+            acc = jnp.concatenate([acc_all[block(b), :HEAD] * shrink, acc_all[block(b), HEAD:] * shrink], axis=1)
+        top_all[block(b), :] = top
+        wide = jnp.concatenate([top] * (KSTEP // 128), axis=1)
+        for k in range(k0, k1, KSTEP):
+            weight = jnp.exp2((s[slot, :, k - k0:k - k0 + KSTEP] - wide).astype(jnp.bfloat16))
+            more = jnp.dot(weight, va[k:k + KSTEP, :], preferred_element_type=jnp.float32)
             acc = more if acc is None else acc + more
-        return here, acc
-
-    def units(b0, b1, block, first=False):
-        def body(b, carry):
-            here, acc = unit(b, block, first)
-            acc_all[here, :] = acc
-            return carry
-
-        lax.fori_loop(b0, b1, body, 0)
+        return acc
+
+    def attend(blocks, keys, fresh=False, done=None):
+        tops = [scores(blocks[0], keys, 0)]
+        for n, b in enumerate(blocks):
+            if n + 1 < len(blocks):
+                tops.append(scores(blocks[n + 1], keys, (n + 1) % 2))
+            acc = mix(b, keys, n % 2, tops[n], fresh)
+            if done is None:
+                acc_all[block(b), :] = acc
+            else:
+                done(b, acc)
 
     def my_columns():
         return pl.ds(pl.multiple_of(me * HEAD, HEAD), HEAD)
@@ -294,8 +325,7 @@
         place_there = (j // 8) * 8 + MIRROR[j % 8]
         return remote(mixed.at[j], out.at[:, my_columns()], os.at[j], orv.at[place_there], owners[j])
 
-    def finish(b):
-        here, acc = unit(b, 3)
+    def finish(b, acc):
         result = (acc[:, :HEAD] / acc[:, HEAD:HEAD + 1]).astype(jnp.bfloat16)
         for n in range(QROWS // TILE):
             j = b * (QROWS // TILE) + n
@@ -376,23 +406,23 @@
     project(6)
     take_z(1)
     take_z(3)
+    keys_step(2)
     project(8)
     take_y(1, CW, 2)
     take_y(1, CCW, 0)
     project(7)
     keys_send(3)
-    keys_step(2)
     project(9)
     keys_send(4)
+    keys_step(3)
     take_y(1, CW, 1)
     take_y(1, CCW, 3)
-    keys_step(3)
+    keys_step(4)
+    attend((0, 1), OWN0, True)
     take_y(1, CW, 4)
     take_y(1, CCW, 4)
-    units(0, 2, 0, True)
     take_y(1, CW, 3)
     take_y(1, CCW, 1)
-    keys_step(4)
     project(10)
     project(11)
     keys_send(5)
@@ -403,24 +433,31 @@
     project(13)
     keys_send(6)
     project(14)
-    project(15)
     keys_send(7)
     keys_step(6)
-    units(2, 4, 0, True)
+    project(15)
+    keys_send(8)
     keys_step(7)
+    attend((2, 3), OWN0, True)
+    keys_step(8)
+    attend((0, 1), OWN1)
+    keys_step(9)
+    keys_step(10)
+    attend((2, 3), OWN1)
+    keys_step(11)
     for ch in range(4):
         keys_take(ch)
-    units(0, 2, 1)
-    keys_step(8)
-    units(2, 4, 1)
-    keys_step(9)
-    units(0, 2, 2)
-    keys_step(10)
-    units(2, 4, 2)
-    for ch in range(4, 8):
+    keys_step(12)
+    attend((0, 1), REF0)
+    keys_step(13)
+    keys_step(14)
+    attend((2, 3), REF0)
+    for ch in (4, 5, 6):
         keys_take(ch)
-    for b in (2, 3, 0, 1):
-        finish(b)
+    attend((0, 1, 2, 3), REF1)
+    for ch in (7, 8):
+        keys_take(ch)
+    attend((2, 3, 0, 1), LAST, done=finish)
     for j in range(1, 16):
         f, dy, cc = logical(j)
         there = out.at[:, pl.ds(pl.multiple_of(shard(f, dy, cc) * HEAD, HEAD), HEAD)]
@@ -464,8 +501,8 @@
             pltpu.VMEM((2 * length, 2 * HEAD), half),
             pltpu.VMEM((length, 2 * HEAD), half),
             pltpu.VMEM((length, 2 * HEAD), half),
-            pieces, pieces, pieces, pieces, pieces, pieces,
-            pltpu.VMEM((QROWS, KROWS), jnp.float32),
+            pieces, pieces, pieces, pieces, pieces, pieces, pieces,
+            pltpu.VMEM((2, QROWS, KROWS), jnp.float32),
             pltpu.VMEM((length, 128), jnp.float32),
             pltpu.VMEM((length, 2 * HEAD), jnp.float32),
             pltpu.VMEM((16, rows, HEAD), half),

time: 127 us -> 120 us (0.945)
  Pallas kernels: 125 us -> 118 us
    pallas_call x1, Pallas kernels: 125 us -> 118 us  [whole_block(): pl.pallas_call(block_kernel, out_shape=jax.ShapeDtypeStruct((rows, 16 * H...]
where the time goes in v3:
time: 120 us
  Pallas kernels  118 us (98%)
  local copies, waits for them, and re-layouts  1.88 us (2%)
    pallas_call x1, Pallas kernels, whole_block(): pl.pallas_call(block_kernel, out_shape=jax.ShapeDtypeStruct((rows, 16 * H...  118 us

profile of v3, /device:TPU:1, one launch (start us, length us, event | category | flops | bytes accessed | tf_op | source)
XLA Modules:
  0.0 119.7 jit_solution(4013327215368883368)
XLA Ops:
  0.0 117.8 %attention_block.1 = bf16[128,2048]{1,0:T(8,128)(2,1)} custom-call(s32[4]{0:T(128)} %references.1, s32[16]{0:T(128)} %pairing.1, s32[16,32]{1,0:T(8,128)} %bitcast.13, bf16[1,384]{1,0:T(2,128)(2,1)} %bias.1, bf16[128,3072]{1,0:T(8,128)(2,1)} %bitcast.10, bf16[3072,384]{1,0:T(8,128)(2,1)} %bitcast.8, bf16[32,3072]{1,0:T(8,128)(2,1)} %bitcast.11, ...), custom_call_target="tpu_custom_call" | custom-call | tf_op jit(solution)/shard_map/attention_block/pallas_call | solution.py:488
  117.9 1.9 %copy.10 = bf16[1,128,2048]{2,1,0:T(8,128)(2,1)} copy(bf16[1,128,2048]{2,1,0:T(8,128)(2,1)} %bitcast.9) | data formatting | bytes 1048576

commit v4 on v3

--- a/solution.py
+++ b/solution.py
@@ -13,7 +13,7 @@
 HALVES = ((0, 1), (2, 3))
 TILE = 128
 HEAD = 128
-SIZES = (2, 2, 2, 2, 2, 2, 2, 1, 1)
+SIZES = (2, 2, 2, 2, 2, 2, 1, 1, 1, 1)
 STARTS = tuple(sum(SIZES[:n]) for n in range(len(SIZES)))
 CHUNKS = len(SIZES)
 LAG = 2
@@ -430,50 +430,53 @@
     take_y(1, CCW, 5)
     keys_step(5)
     project(12)
+    keys_send(6)
     project(13)
-    keys_send(6)
-    project(14)
     keys_send(7)
     keys_step(6)
-    project(15)
+    project(14)
     keys_send(8)
     keys_step(7)
+    project(15)
+    keys_send(9)
+    keys_step(8)
     attend((2, 3), OWN0, True)
-    keys_step(8)
-    attend((0, 1), OWN1)
     keys_step(9)
     keys_step(10)
+    attend((0, 1), OWN1)
+    keys_step(11)
+    keys_step(12)
     attend((2, 3), OWN1)
-    keys_step(11)
+    keys_step(13)
     for ch in range(4):
         keys_take(ch)
-    keys_step(12)
+    keys_step(14)
+    keys_step(15)
     attend((0, 1), REF0)
-    keys_step(13)
-    keys_step(14)
     attend((2, 3), REF0)
-    for ch in (4, 5, 6):
+    for ch in (4, 5, 6, 7):
         keys_take(ch)
     attend((0, 1, 2, 3), REF1)
-    for ch in (7, 8):
+    for ch in (8, 9):
         keys_take(ch)
     attend((2, 3, 0, 1), LAST, done=finish)
+    for copy in started:
+        copy.wait_send()
+
+    @pl.when(zl < 3)
+    def _():
+        for ch in range(CHUNKS):
+            r_copy(ch).wait_send()
+
+    @pl.when(zl > 0)
+    def _():
+        for ch in range(CHUNKS):
+            l_copy(ch).wait_send()
+
     for j in range(1, 16):
         f, dy, cc = logical(j)
         there = out.at[:, pl.ds(pl.multiple_of(shard(f, dy, cc) * HEAD, HEAD), HEAD)]
         remote(there, there, os.at[j], orv.at[j], owners[j]).wait_recv()
-    for copy in started:
-        copy.wait_send()
-
-    @pl.when(zl < 3)
-    def _():
-        for ch in range(CHUNKS):
-            r_copy(ch).wait_send()
-
-    @pl.when(zl > 0)
-    def _():
-        for ch in range(CHUNKS):
-            l_copy(ch).wait_send()
 
 
 def whole_block(references, pairing, mask, bias, tok, w, down, up):

time: 120 us -> 118 us (0.983)
  Pallas kernels: 118 us -> 116 us
    pallas_call x1, Pallas kernels: 118 us -> 116 us  [whole_block(): pl.pallas_call(block_kernel, out_shape=jax.ShapeDtypeStruct((rows, 16 * H...]
where the time goes in v4:
time: 118 us
  Pallas kernels  116 us (98%)
  local copies, waits for them, and re-layouts  1.88 us (2%)
    pallas_call x1, Pallas kernels, whole_block(): pl.pallas_call(block_kernel, out_shape=jax.ShapeDtypeStruct((rows, 16 * H...  116 us

profile of v4, /device:TPU:1, one launch (start us, length us, event | category | flops | bytes accessed | tf_op | source)
XLA Modules:
  0.0 118.2 jit_solution(13323841512323915666)
XLA Ops:
  0.0 116.4 %attention_block.1 = bf16[128,2048]{1,0:T(8,128)(2,1)} custom-call(s32[4]{0:T(128)} %references.1, s32[16]{0:T(128)} %pairing.1, s32[16,32]{1,0:T(8,128)} %bitcast.13, bf16[1,384]{1,0:T(2,128)(2,1)} %bias.1, bf16[128,3072]{1,0:T(8,128)(2,1)} %bitcast.10, bf16[3072,384]{1,0:T(8,128)(2,1)} %bitcast.8, bf16[32,3072]{1,0:T(8,128)(2,1)} %bitcast.11, ...), custom_call_target="tpu_custom_call" | custom-call | tf_op jit(solution)/shard_map/attention_block/pallas_call | solution.py:491
  116.4 1.9 %copy.10 = bf16[1,128,2048]{2,1,0:T(8,128)(2,1)} copy(bf16[1,128,2048]{2,1,0:T(8,128)(2,1)} %bitcast.9) | data formatting | bytes 1048576

commit v5 on v4

--- a/solution.py
+++ b/solution.py
@@ -450,10 +450,10 @@
     keys_step(13)
     for ch in range(4):
         keys_take(ch)
+    attend((0, 1), REF0)
     keys_step(14)
+    attend((2, 3), REF0)
     keys_step(15)
-    attend((0, 1), REF0)
-    attend((2, 3), REF0)
     for ch in (4, 5, 6, 7):
         keys_take(ch)
     attend((0, 1, 2, 3), REF1)

time: 118 us -> 119 us (level)
  no operation moved by 1% of the time
where the time goes in v5:
time: 119 us
  Pallas kernels  117 us (98%)
  local copies, waits for them, and re-layouts  1.88 us (2%)
    pallas_call x1, Pallas kernels, whole_block(): pl.pallas_call(block_kernel, out_shape=jax.ShapeDtypeStruct((rows, 16 * H...  117 us

profile of v5, /device:TPU:1, one launch (start us, length us, event | category | flops | bytes accessed | tf_op | source)
XLA Modules:
  0.0 118.6 jit_solution(8463717810760599247)
XLA Ops:
  0.0 116.7 %attention_block.1 = bf16[128,2048]{1,0:T(8,128)(2,1)} custom-call(s32[4]{0:T(128)} %references.1, s32[16]{0:T(128)} %pairing.1, s32[16,32]{1,0:T(8,128)} %bitcast.13, bf16[1,384]{1,0:T(2,128)(2,1)} %bias.1, bf16[128,3072]{1,0:T(8,128)(2,1)} %bitcast.10, bf16[3072,384]{1,0:T(8,128)(2,1)} %bitcast.8, bf16[32,3072]{1,0:T(8,128)(2,1)} %bitcast.11, ...), custom_call_target="tpu_custom_call" | custom-call | tf_op jit(solution)/shard_map/attention_block/pallas_call | solution.py:491
  116.7 1.9 %copy.10 = bf16[1,128,2048]{2,1,0:T(8,128)(2,1)} copy(bf16[1,128,2048]{2,1,0:T(8,128)(2,1)} %bitcast.9) | data formatting | bytes 1048576
